TPU v7x, 512 devices: a whole 4x4x16 slice. The times are simulated.
512 devices in a mesh: req: 64 (over y, z), tp: 8 (over x, core).
Axes of the slice: x: 4, y: 4, z: 16, core: 2. Of those that a mesh axis runs over, the one named last changes fastest.
Arguments:
- tail_queries: bfloat16 [128, 256, 64, 128], P('req', None, 'tp'), may hold values from -140 to 140
- tail_keys: bfloat16 [128, 256, 8, 128], P('req', 'tp'), may hold values from -6 to 6
- tail_values: bfloat16 [128, 256, 8, 128], P('req', 'tp'), may hold values from -6 to 6
- prefix_keys: bfloat16 [128, 768, 8, 128], P('req', None, 'tp'), may hold values from -4 to 4
- prefix_values: bfloat16 [128, 768, 8, 128], P('req', None, 'tp'), may hold values from -6 to 6
- decode_queries: bfloat16 [128, 4, 64, 128], P('req', None, 'tp'), may hold values from -140 to 140
- decode_keys: bfloat16 [128, 4, 8, 128], P('req', None, 'tp'), may hold values from -6 to 6
- decode_values: bfloat16 [128, 4, 8, 128], P('req', None, 'tp'), may hold values from -6 to 6
- prompt_lengths: int32 [128], P('req'), may hold values from 258 to 1024, as said below
- block_dest: int32 [128, 64, 1], P('req'), may hold values from 0 to 63; in each aligned block of 128 rows (0 to 127, 128 to 255, ..., all dimensions but the last counted through in order) at most 4 rows name the same one
Outputs:
- prefill_out: bfloat16 [128, 256, 64, 128], P('req', None, 'tp')
- decode_out: bfloat16 [128, 4, 64, 128], P('req', None, 'tp')
- pool_keys: bfloat16 [64, 256, 16, 8, 128], P('req', None, None, 'tp')
- pool_values: bfloat16 [64, 256, 16, 8, 128], P('req', None, None, 'tp')
Inputs may be any that keep to these rules, and one draw needn't show every extreme that they name: `prompt_lengths`: some prompt has exactly 1024 tokens and some exactly 258. `block_dest`: among the 128 blocks of one request group, no pool group is named more than 4 times.
All inputs are finite; a program needn't handle non-finite values.
Results may differ from a plain program's by a relative error of at most 0.0046.
Values may be sent and summed in bfloat16 or wider, within the bound.
A program may use at most 64 MiB of HBM per device.

v0:
```python
import math

import jax
import jax.numpy as jnp
from jax import lax
from jax.sharding import PartitionSpec as P

BLOCK = 16


def assemble(prefix, tail_part, length):
    tail_len = tail_part.shape[0]
    zero_rows = jnp.zeros((tail_len,) + prefix.shape[1:], prefix.dtype)
    padded = jnp.concatenate([prefix, zero_rows], 0)
    placed = lax.dynamic_update_slice_in_dim(padded, tail_part, length - tail_len, 0)
    position = jnp.arange(padded.shape[0], dtype=jnp.int32)
    return jnp.where((position < length)[:, None, None], placed, jnp.zeros_like(placed))


def prefill_one(queries, key_rows, value_rows, length):
    tail_len, head_count, head_size = queries.shape
    kv_heads = key_rows.shape[1]
    shaped = queries.reshape(tail_len, kv_heads, head_count // kv_heads, head_size)
    scores = jnp.einsum("tkgd,skd->kgts", shaped, key_rows, preferred_element_type=jnp.float32) * (
        1.0 / math.sqrt(head_size)
    )
    last_seen = length - tail_len + jnp.arange(tail_len, dtype=jnp.int32)
    visible = jnp.arange(key_rows.shape[0], dtype=jnp.int32)[None, :] <= last_seen[:, None]
    scores = jnp.where(visible, scores, -jnp.inf)
    row_peak = jnp.max(scores, -1, keepdims=True)
    weights = jnp.exp(scores - row_peak)
    weight_sum = jnp.sum(weights, -1)
    summed = jnp.einsum(
        "kgts,skd->tkgd",
        weights.astype(jnp.bfloat16),
        value_rows,
        preferred_element_type=jnp.float32,
    )
    result = summed / jnp.transpose(weight_sum, (2, 0, 1))[..., None]
    return result.reshape(tail_len, head_count, head_size).astype(jnp.bfloat16)


def fresh_terms(shaped, new_keys):
    steps = shaped.shape[0]
    scores = jnp.einsum("qkgd,nkd->kgqn", shaped, new_keys, preferred_element_type=jnp.float32) * (
        1.0 / math.sqrt(shaped.shape[3])
    )
    causal = jnp.arange(steps)[None, :] <= jnp.arange(steps)[:, None]
    return jnp.where(causal, scores, -jnp.inf)


def decode_owner(queries, key_rows, value_rows, new_keys, new_values, length):
    steps, head_count, head_size = queries.shape
    kv_heads = key_rows.shape[1]
    shaped = queries.reshape(steps, kv_heads, head_count // kv_heads, head_size)
    prompt_scores = jnp.einsum(
        "qkgd,skd->kgqs", shaped, key_rows, preferred_element_type=jnp.float32
    ) * (1.0 / math.sqrt(head_size))
    prompt_scores = jnp.where(
        jnp.arange(key_rows.shape[0], dtype=jnp.int32) < length, prompt_scores, -jnp.inf
    )
    fresh_scores = fresh_terms(shaped, new_keys)
    row_peak = jnp.maximum(jnp.max(prompt_scores, -1), jnp.max(fresh_scores, -1))[..., None]
    prompt_weights = jnp.exp(prompt_scores - row_peak)
    fresh_weights = jnp.exp(fresh_scores - row_peak)
    weight_sum = jnp.sum(prompt_weights, -1) + jnp.sum(fresh_weights, -1)
    summed = jnp.einsum(
        "kgqs,skd->kgqd",
        prompt_weights.astype(jnp.bfloat16),
        value_rows,
        preferred_element_type=jnp.float32,
    )
    summed = summed + jnp.einsum(
        "kgqn,nkd->kgqd",
        fresh_weights.astype(jnp.bfloat16),
        new_values,
        preferred_element_type=jnp.float32,
    )
    result = summed / weight_sum[..., None]
    return (
        jnp.transpose(result, (2, 0, 1, 3))
        .reshape(steps, head_count, head_size)
        .astype(jnp.bfloat16)
    )


def per_device(
    tail_queries,
    tail_keys,
    tail_values,
    prefix_keys,
    prefix_values,
    decode_queries,
    decode_keys,
    decode_values,
    prompt_lengths,
    block_dest,
):
    groups_count = lax.axis_size("req")
    prompts_here, tail_len, head_count, head_size = tail_queries.shape
    kv_heads = prefix_keys.shape[2]
    tail_k, tail_v = (
        lax.all_to_all(tail_keys, "tp", split_axis=2, concat_axis=1, tiled=True),
        lax.all_to_all(tail_values, "tp", split_axis=2, concat_axis=1, tiled=True),
    )
    whole_k = jax.vmap(assemble)(prefix_keys, tail_k, prompt_lengths)
    whole_v = jax.vmap(assemble)(prefix_values, tail_v, prompt_lengths)
    blocks_per = whole_k.shape[1] // BLOCK
    per_source = prompts_here * blocks_per
    capacity = max(2, 2 * per_source // groups_count)
    slot_count = groups_count * capacity
    target = block_dest.reshape(per_source)
    onehot = (target[:, None] == jnp.arange(groups_count, dtype=jnp.int32)[None, :]).astype(
        jnp.int32
    )
    block_rank = jnp.sum((jnp.cumsum(onehot, 0) - onehot) * onehot, 1)
    send_slot = target * capacity + block_rank

    def pack(whole):
        blocks = whole.reshape(per_source, BLOCK, kv_heads, head_size)
        empty_slots = jnp.zeros((slot_count, BLOCK, kv_heads, head_size), whole.dtype)
        return (
            empty_slots.at[send_slot]
            .set(blocks)
            .reshape(groups_count, capacity, BLOCK, kv_heads, head_size)
        )

    pool_k, pool_v = (
        lax.all_to_all(pack(whole_k), "req", split_axis=0, concat_axis=0, tiled=True),
        lax.all_to_all(pack(whole_v), "req", split_axis=0, concat_axis=0, tiled=True),
    )

    def prefill_item(items):
        return prefill_one(items[0], items[1], items[2], items[3])

    prefill_out = lax.map(prefill_item, (tail_queries, whole_k, whole_v, prompt_lengths))

    def decode_item(items):
        return decode_owner(items[0], items[1], items[2], items[3], items[4], items[5])

    decode_out = lax.map(
        decode_item, (decode_queries, whole_k, whole_v, decode_keys, decode_values, prompt_lengths)
    )
    pool_keys = pool_k.reshape(1, slot_count, BLOCK, kv_heads, head_size)
    pool_values = pool_v.reshape(1, slot_count, BLOCK, kv_heads, head_size)
    return (prefill_out, decode_out, pool_keys, pool_values)


def solution(mesh):
    in_specs = (
        P("req", None, "tp", None),
        P("req", "tp", None, None),
        P("req", "tp", None, None),
        P("req", None, "tp", None),
        P("req", None, "tp", None),
        P("req", None, "tp", None),
        P("req", None, "tp", None),
        P("req", None, "tp", None),
        P("req"),
        P("req", None, None),
    )
    out_specs = (
        P("req", None, "tp", None),
        P("req", None, "tp", None),
        P("req", None, None, "tp", None),
        P("req", None, None, "tp", None),
    )
    return jax.shard_map(
        per_device, mesh=mesh, in_specs=in_specs, out_specs=out_specs, check_vma=False
    )
```

profile of v0, /device:TPU:24, one launch (start us, length us, event | category | flops | bytes accessed | tf_op | source)
XLA Modules:
  0.0 204.8 jit_solution(14500613928534151198)
XLA Ops:
  2.2 4.3 %all-to-all-start.1 = ((bf16[2,32,8,128]{3,1,0,2:T(8,128)(2,1)}), bf16[2,32,8,128]{3,1,0,2:T(8,128)(2,1)S(1)}, u32[]{:S(2)}, u32[]{:S(2)}) async-start(bf16[2,32,8,128]{3,1,0,2:T(8,128)(2,1)} %copy.58), calls=%async_computation.1 | async-start | bytes 262144 | tf_op jit(solution)/shard_map/all_to_all | solution.py:103
  10.3 2.5 %copy.51 = bf16[2,768,1,128]{3,2,1,0:T(2,128)(2,1)} copy(bf16[2,768,1,128]{3,1,2,0:T(8,128)(2,1)} %param.18) | data formatting | bytes 786432 | tf_op args[4]
  17.7 2.1 %concatenate.10 = bf16[2,1024,1,128]{3,2,1,0:T(2,128)(2,1)S(1)} pad(bf16[2,768,1,128]{3,2,1,0:T(2,128)(2,1)} %copy.51, bf16[]{:T(256)} %constant.85.clone.1), padding=0_0x0_256x0_0x0_0 | pad | bytes 917506 | tf_op jit(solution)/shard_map/vmap()/concatenate | solution.py:14
  19.9 4.8 %all-to-all-start = ((bf16[2,32,8,128]{3,1,0,2:T(8,128)(2,1)}), bf16[2,32,8,128]{3,1,0,2:T(8,128)(2,1)S(1)}, u32[]{:S(2)}, u32[]{:S(2)}) async-start(bf16[2,32,8,128]{3,1,0,2:T(8,128)(2,1)} %copy.52), calls=%async_computation | async-start | bytes 262144 | tf_op jit(solution)/shard_map/all_to_all | solution.py:104
  24.7 13.2 %while.27 = (s32[]{:T(128)}, bf16[2,1024,1,128]{3,2,1,0:T(2,128)(2,1)S(1)}, s32[2,4]{1,0:T(2,128)S(1)}, bf16[2,256,1,128]{3,1,0,2:T(8,128)(2,1)S(1)}, s32[]{:T(128)}, /*index=5*/s32[4]{0:T(128)}) while((s32[]{:T(128)}, bf16[2,1024,1,128]{3,2,1,0:T(2,128)(2,1)S(1)}, s32[2,4]{1,0:T(2,128)S(1)}, bf16[2,256,1,128]{3,1,0,2:T(8,128)(2,1)S(1)}, s32[]{:T(128)}, ...), condition=%wide.while_cond.1, body=%wide.while_body.1.sunk | while | flops 32797 | bytes 458943 | solution.py:15
  25.4 3.9 %and_reduce_fusion.5 = pred[]{:T(512)} fusion(s32[4]{0:T(128)} %get-tuple-element.462, s32[1]{0:T(128)} %bitcast.234, s32[1]{0:T(128)} %bitcast.235, s32[1]{0:T(128)} %bitcast.236, s32[1]{0:T(128)} %bitcast.237), kind=kLoop, calls=%fused_computation.74.clone.1 | loop fusion | flops 27 | bytes 33 | tf_op jit(solution)/shard_map/vmap(vmap())/scatter
  32.0 3.9 %and_reduce_fusion.5 = pred[]{:T(512)} fusion(s32[4]{0:T(128)} %get-tuple-element.462, s32[1]{0:T(128)} %bitcast.234, s32[1]{0:T(128)} %bitcast.235, s32[1]{0:T(128)} %bitcast.236, s32[1]{0:T(128)} %bitcast.237), kind=kLoop, calls=%fused_computation.74.clone.1 | loop fusion | flops 27 | bytes 33 | tf_op jit(solution)/shard_map/vmap(vmap())/scatter
  38.0 13.3 %while.26 = (s32[]{:T(128)}, bf16[2,1024,1,128]{3,2,1,0:T(2,128)(2,1)S(1)}, s32[2,4]{1,0:T(2,128)S(1)}, bf16[2,256,1,128]{3,1,0,2:T(8,128)(2,1)S(1)}, s32[]{:T(128)}, /*index=5*/s32[4]{0:T(128)}) while((s32[]{:T(128)}, bf16[2,1024,1,128]{3,2,1,0:T(2,128)(2,1)S(1)}, s32[2,4]{1,0:T(2,128)S(1)}, bf16[2,256,1,128]{3,1,0,2:T(8,128)(2,1)S(1)}, s32[]{:T(128)}, ...), condition=%wide.while_cond, body=%wide.while_body.sunk | while | flops 32797 | bytes 458943 | solution.py:15
  38.6 3.9 %and_reduce_fusion.4 = pred[]{:T(512)} fusion(s32[4]{0:T(128)} %get-tuple-element.480, s32[1]{0:T(128)} %bitcast.228, s32[1]{0:T(128)} %bitcast.229, s32[1]{0:T(128)} %bitcast.230, s32[1]{0:T(128)} %bitcast.231), kind=kLoop, calls=%fused_computation.69.clone.1 | loop fusion | flops 27 | bytes 33 | tf_op jit(solution)/shard_map/vmap(vmap())/scatter
  42.5 2.0 %fusion.105 = bf16[2,1024,1,128]{3,2,1,0:T(2,128)(2,1)S(1)} fusion(bf16[2,1024,1,128]{3,2,1,0:T(2,128)(2,1)S(1)} %get-tuple-element.470, s32[]{:T(128)} %bitcast.226, s32[]{:T(128)} %bitcast.227, pred[]{:T(512)} %and_reduce_fusion.4, bf16[1,256,1,128]{3,1,0,2:T(8,128)(2,1)S(1)} %constant_dynamic-slice_fusion.14), kind=kLoop, calls=%fused_computation.68.clone.1 | loop fusion | flops 32768 | bytes 327689 | tf_op jit(solution)/shard_map/vmap(vmap())/scatter
  45.2 3.9 %and_reduce_fusion.4 = pred[]{:T(512)} fusion(s32[4]{0:T(128)} %get-tuple-element.480, s32[1]{0:T(128)} %bitcast.228, s32[1]{0:T(128)} %bitcast.229, s32[1]{0:T(128)} %bitcast.230, s32[1]{0:T(128)} %bitcast.231), kind=kLoop, calls=%fused_computation.69.clone.1 | loop fusion | flops 27 | bytes 33 | tf_op jit(solution)/shard_map/vmap(vmap())/scatter
  49.2 2.0 %fusion.105 = bf16[2,1024,1,128]{3,2,1,0:T(2,128)(2,1)S(1)} fusion(bf16[2,1024,1,128]{3,2,1,0:T(2,128)(2,1)S(1)} %get-tuple-element.470, s32[]{:T(128)} %bitcast.226, s32[]{:T(128)} %bitcast.227, pred[]{:T(512)} %and_reduce_fusion.4, bf16[1,256,1,128]{3,1,0,2:T(8,128)(2,1)S(1)} %constant_dynamic-slice_fusion.14), kind=kLoop, calls=%fused_computation.68.clone.1 | loop fusion | flops 32768 | bytes 327689 | tf_op jit(solution)/shard_map/vmap(vmap())/scatter
  52.8 13.2 %scatter_fusion = bf16[256,16,128]{2,1,0:T(8,128)(2,1)} fusion(bf16[256,16,128]{2,1,0:T(8,128)(2,1)} %broadcast.152.clone, s32[128]{0:T(128)S(1)} %fusion.61, bf16[128,16,128]{2,1,0:T(8,128)(2,1)S(1)} %bitcast.238), kind=kCustom, calls=%fused_computation | custom fusion | bytes 1573376 | tf_op jit(solution)/shard_map/scatter | solution.py:124
  66.0 18.7 %all-to-all-start.2 = ((bf16[64,4,16,1,128]{4,2,1,3,0:T(8,128)(2,1)}), bf16[64,4,16,1,128]{4,2,1,3,0:T(8,128)(2,1)S(1)}, u32[]{:S(2)}, u32[]{:S(2)}) async-start(bf16[64,4,16,1,128]{4,2,1,3,0:T(8,128)(2,1)} %bitcast.47), calls=%async_computation.2 | async-start | bytes 2097152 | tf_op jit(solution)/shard_map/all_to_all | solution.py:129
  85.9 13.2 %scatter_fusion.1 = bf16[256,16,128]{2,1,0:T(8,128)(2,1)} fusion(bf16[256,16,128]{2,1,0:T(8,128)(2,1)} %broadcast.152.clone.1, s32[128]{0:T(128)S(1)} %fusion.61, bf16[128,16,128]{2,1,0:T(8,128)(2,1)S(1)} %bitcast.240), kind=kCustom, calls=%fused_computation.1 | custom fusion | bytes 1573376 | tf_op jit(solution)/shard_map/scatter | solution.py:124
  99.1 5.2 %while.25 = (s32[]{:T(128)}, bf16[2,4,8,128]{3,2,1,0:T(8,128)(2,1)S(1)}, s32[2]{0:T(128)S(1)}, bf16[2,1024,1,128]{3,1,2,0:T(8,128)(2,1)S(1)}, bf16[2,4,8,128]{3,...) while((s32[]{:T(128)}, ...), condition=%wide.region_11.12_spmd, body=%wide.region_6.11_spmd.sunk | while | flops 17086288 | bytes 993705 | solution.py:141
  104.3 35.1 %all-to-all-done.2 = bf16[64,4,16,1,128]{4,2,1,3,0:T(8,128)(2,1)S(1)} async-done(((bf16[64,4,16,1,128]{4,2,1,3,0:T(8,128)(2,1)}), bf16[64,4,16,1,128]{4,2,1,3,0:T(8,128)(2,1)S(1)}, u32[]{:S(2)}, u32[]{:S(2)}) %all-to-all-start.2) | async-done | bytes 1048608 | tf_op jit(solution)/shard_map/all_to_all | solution.py:129
  139.4 6.8 %all-to-all-start.3 = ((bf16[64,4,16,1,128]{4,2,1,3,0:T(8,128)(2,1)}), bf16[64,4,16,1,128]{4,2,1,3,0:T(8,128)(2,1)}, u32[]{:S(2)}, u32[]{:S(2)}) async-start(bf16[64,4,16,1,128]{4,2,1,3,0:T(8,128)(2,1)} %bitcast.51), calls=%async_computation.3 | async-start | bytes 2097152 | tf_op jit(solution)/shard_map/all_to_all | solution.py:130
  146.3 15.8 %while.24 = (s32[]{:T(128)}, bf16[2,256,8,128]{3,2,1,0:T(8,128)(2,1)}, bf16[2,1024,1,128]{3,1,0,2:T(8,128)(2,1)S(1)}, s32[2]{0:T(128)S(1)}, bf16[2,1024,1,128]{3...) while((s32[]{:T(128)}, bf16[2,256,8,128]{3,2,1,0:T(8,128)(2,1)}, ...), condition=%wide.region_5.6_spmd, body=%wide.region_2.5_spmd.sunk | while | flops 1097593088 | bytes 30976136 | solution.py:136
  150.8 2.2 %fusion.91 = bf16[1,256,8,128]{1,3,2,0:T(8,128)(2,1)S(1)} fusion(f32[1024,256,8]{1,0,2:T(8,128)S(1)} %get-tuple-element.415, f32[8,256]{1,0:T(8,128)S(1)} %get-tuple-element.416, pred[256,1024]{0,1:T(8,128)(4,1)S(1)} %iota_compare_fusion.8, f32[256,8]{0,1:T(8,128)S(1)} %bitcast.246, bf16[2,1024,1,128]{3,1,0,2:T(8,128)(2,1)S(1)} %get-tuple-element.499, ...), kind=kOutput, calls=%fused_computation.13.clone.1 | convolution fusion | flops 545783808 | bytes 9453572 | tf_op jit(solution)/shard_map/while/body/eval_jaxpr/kgts,skd->tkgd/dot_general | solution.py:33
  158.7 2.2 %fusion.91 = bf16[1,256,8,128]{1,3,2,0:T(8,128)(2,1)S(1)} fusion(f32[1024,256,8]{1,0,2:T(8,128)S(1)} %get-tuple-element.415, f32[8,256]{1,0:T(8,128)S(1)} %get-tuple-element.416, pred[256,1024]{0,1:T(8,128)(4,1)S(1)} %iota_compare_fusion.8, f32[256,8]{0,1:T(8,128)S(1)} %bitcast.246, bf16[2,1024,1,128]{3,1,0,2:T(8,128)(2,1)S(1)} %get-tuple-element.499, ...), kind=kOutput, calls=%fused_computation.13.clone.1 | convolution fusion | flops 545783808 | bytes 9453572 | tf_op jit(solution)/shard_map/while/body/eval_jaxpr/kgts,skd->tkgd/dot_general | solution.py:33
  162.0 38.1 %all-to-all-done.3 = bf16[64,4,16,1,128]{4,2,1,3,0:T(8,128)(2,1)} async-done(((bf16[64,4,16,1,128]{4,2,1,3,0:T(8,128)(2,1)}), bf16[64,4,16,1,128]{4,2,1,3,0:T(8,128)(2,1)}, u32[]{:S(2)}, u32[]{:S(2)}) %all-to-all-start.3) | async-done | bytes 1048608 | tf_op jit(solution)/shard_map/all_to_all | solution.py:130
  200.1 2.4 %copy.148 = bf16[1,256,16,1,128]{4,2,3,1,0:T(8,128)(2,1)} copy(bf16[1,256,16,1,128]{4,2,3,1,0:T(8,128)(2,1)} %bitcast.243) | data formatting | bytes 2097152
  202.5 2.4 %copy.149 = bf16[1,256,16,1,128]{4,2,3,1,0:T(8,128)(2,1)} copy(bf16[1,256,16,1,128]{4,2,3,1,0:T(8,128)(2,1)} %bitcast.53) | data formatting | bytes 2097152
  (95 shorter events, 34.9 us)
Async XLA Ops:
  2.2 17.7 %all-to-all-start.1 = ((bf16[2,32,8,128]{3,1,0,2:T(8,128)(2,1)}), bf16[2,32,8,128]{3,1,0,2:T(8,128)(2,1)S(1)}, u32[]{:S(2)}, u32[]{:S(2)}) async-start(bf16[2,32,8,128]{3,1,0,2:T(8,128)(2,1)} %copy.58), calls=%async_computation.1 | async-start | bytes 262144 | tf_op jit(solution)/shard_map/all_to_all | solution.py:103
  19.8 79.2 %copy-start.2 = (bf16[2,4,8,128]{3,2,1,0:T(8,128)(2,1)S(1)}, bf16[2,4,8,128]{3,2,1,0:T(8,128)(2,1)}, u32[]{:S(2)}) copy-start(bf16[2,4,8,128]{3,2,1,0:T(8,128)(2,1)} %param.19) | copy-start | bytes 49156
  19.8 79.2 %copy-start.3 = (bf16[2,4,1,128]{3,1,2,0:T(4,128)(2,1)S(1)}, bf16[2,4,1,128]{3,1,2,0:T(4,128)(2,1)}, u32[]{:S(2)}) copy-start(bf16[2,4,1,128]{3,1,2,0:T(4,128)(2,1)} %param.20) | copy-start | bytes 6148
  19.8 79.2 %copy-start.4 = (s32[2]{0:T(128)S(1)}, s32[2]{0:T(128)}, u32[]{:S(2)}) copy-start(s32[2]{0:T(128)} %param.22) | copy-start | bytes 28
  19.8 79.2 %copy-start.5 = (bf16[2,4,1,128]{3,1,2,0:T(4,128)(2,1)S(1)}, bf16[2,4,1,128]{3,1,2,0:T(4,128)(2,1)}, u32[]{:S(2)}) copy-start(bf16[2,4,1,128]{3,1,2,0:T(4,128)(2,1)} %param.21) | copy-start | bytes 6148
  19.9 18.0 %all-to-all-start = ((bf16[2,32,8,128]{3,1,0,2:T(8,128)(2,1)}), bf16[2,32,8,128]{3,1,0,2:T(8,128)(2,1)S(1)}, u32[]{:S(2)}, u32[]{:S(2)}) async-start(bf16[2,32,8,128]{3,1,0,2:T(8,128)(2,1)} %copy.52), calls=%async_computation | async-start | bytes 262144 | tf_op jit(solution)/shard_map/all_to_all | solution.py:104
  51.7 94.5 %copy-start = (bf16[2,256,8,128]{3,2,1,0:T(8,128)(2,1)S(1)}, bf16[2,256,8,128]{3,2,1,0:T(8,128)(2,1)}, u32[]{:S(2)}) copy-start(bf16[2,256,8,128]{3,2,1,0:T(8,128)(2,1)} %param.14) | copy-start | bytes 3145732
  66.0 73.4 %all-to-all-start.2 = ((bf16[64,4,16,1,128]{4,2,1,3,0:T(8,128)(2,1)}), bf16[64,4,16,1,128]{4,2,1,3,0:T(8,128)(2,1)S(1)}, u32[]{:S(2)}, u32[]{:S(2)}) async-start(bf16[64,4,16,1,128]{4,2,1,3,0:T(8,128)(2,1)} %bitcast.47), calls=%async_computation.2 | async-start | bytes 2097152 | tf_op jit(solution)/shard_map/all_to_all | solution.py:129
  104.3 42.0 %copy-start.6 = (bf16[2,4,8,128]{3,2,1,0:T(8,128)(2,1)}, bf16[2,4,8,128]{3,2,1,0:T(8,128)(2,1)S(1)}, u32[]{:S(2)}) copy-start(bf16[2,4,8,128]{3,2,1,0:T(8,128)(2,1)S(1)} %get-tuple-element.537) | copy-start | bytes 49156
  139.4 6.9 %copy-start.1 = (bf16[64,4,16,1,128]{4,2,1,3,0:T(8,128)(2,1)}, bf16[64,4,16,1,128]{4,2,1,3,0:T(8,128)(2,1)S(1)}, u32[]{:S(2)}) copy-start(bf16[64,4,16,1,128]{4,2,1,3,0:T(8,128)(2,1)S(1)} %all-to-all-done.2) | copy-start | bytes 3145732
  139.4 60.7 %all-to-all-start.3 = ((bf16[64,4,16,1,128]{4,2,1,3,0:T(8,128)(2,1)}), bf16[64,4,16,1,128]{4,2,1,3,0:T(8,128)(2,1)}, u32[]{:S(2)}, u32[]{:S(2)}) async-start(bf16[64,4,16,1,128]{4,2,1,3,0:T(8,128)(2,1)} %bitcast.51), calls=%async_computation.3 | async-start | bytes 2097152 | tf_op jit(solution)/shard_map/all_to_all | solution.py:130
where the time goes:
time: 207 us; the launch traced here: 205 us
  waiting for transfers between devices  73.2 us (35%)
  local copies, waits for them, and re-layouts  51.8 us (25%)
  starting transfers between devices  34.7 us (17%)
  other arithmetic  34.2 us (17%)
  matrix products  8.74 us (4%)
    all_to_all x1, waiting for transfers between devices, per_device(): lax.all_to_all(pack(whole_v), 'req', split_axis=0, concat_axis=0, tiled=T...  38.1 us
    all_to_all x1, waiting for transfers between devices, per_device(): lax.all_to_all(pack(whole_k), 'req', split_axis=0, concat_axis=0, tiled=T...  35.1 us
    scatter x2, local copies, waits for them, and re-layouts, pack(): return empty_slots.at[send_slot].set(blocks).reshape(groups_count, capaci...  26.4 us
    scatter x8, other arithmetic  23.9 us
    all_to_all x1, starting transfers between devices, per_device(): lax.all_to_all(pack(whole_k), 'req', split_axis=0, concat_axis=0, tiled=T...  18.7 us
    unnamed x23, local copies, waits for them, and re-layouts  12.6 us
    all_to_all x1, starting transfers between devices, per_device(): lax.all_to_all(pack(whole_v), 'req', split_axis=0, concat_axis=0, tiled=T...  6.82 us
    all_to_all x1, starting transfers between devices, per_device(): lax.all_to_all(tail_values, 'tp', split_axis=2, concat_axis=1, tiled=True)  4.82 us
  transfers between devices with their start and end apart: 4, of which 2 were waited for; matrix products, arithmetic and copies ran while one was open for 29% of the time, Pallas kernels for 0%

commit v1 on v0

v1 whole, which is shorter than its diff:
```python
import functools
import math

import jax
import jax.numpy as jnp
from jax import lax
from jax.experimental import pallas as pl
from jax.experimental.pallas import tpu as pltpu
from jax.sharding import PartitionSpec as P

MESH = pl.DeviceIdType.MESH
BLOCK = 16
SLOTS = 4
Y = 4
F32 = jnp.float32
BF16 = jnp.bfloat16


def iota(shape, dim):
    return lax.broadcasted_iota(jnp.int32, shape, dim)


def dot(a, b):
    return jnp.dot(a, b, preferred_element_type=F32)


def dot_t(a, b):
    return lax.dot_general(a, b, (((1,), (1,)), ((), ())), preferred_element_type=F32)


def slot_table(dest_row, slots, empty):
    count = dest_row.shape[1]
    by_lane = jnp.broadcast_to(dest_row, (count, count))
    by_row = by_lane.T
    earlier = iota((count, count), 1) < iota((count, count), 0)
    rank = jnp.sum(jnp.where((by_lane == by_row) & earlier, 1, 0), axis=1, keepdims=True)
    slot = by_row[:, :1] * SLOTS + rank
    held = slot == iota((count, slots), 1)
    block = iota((count, slots), 0) - empty
    return jnp.sum(jnp.where(held, block, 0), axis=0, keepdims=True) + empty


def exchange_kernel(
    groups,
    heads,
    tk_in,
    tv_in,
    dest_in,
    len_in,
    pk_in,
    pv_in,
    q_in,
    dq_in,
    dk_in,
    dv_in,
    out_ref,
    dout_ref,
    pool_ref,
    tk_ref,
    tv_ref,
    dest_ref,
    len_ref,
    pk_ref,
    pv_ref,
    q_ref,
    dq_ref,
    dk_ref,
    dv_ref,
    tsend,
    trecv,
    tail,
    wk,
    wv,
    send,
    tab_v,
    tab_s,
    tail_ssem,
    tail_rsem,
    ssem,
    rsem,
    lsem,
    isem,
):
    prompts, tail_len, group, hd = q_ref.shape
    tokens = tk_ref.shape[1]
    prefix_len = pk_ref.shape[1]
    whole_len = prefix_len + tail_len
    per_prompt = whole_len // BLOCK
    blocks = prompts * per_prompt
    me = lax.axis_index("req")
    tp = lax.axis_index("tp")
    nz = groups // Y
    my_y, my_z = me // nz, me % nz

    def partner(d):
        return lax.rem(my_y + d // nz, Y) * nz + lax.rem(my_z + d % nz, nz)

    loads = [
        pltpu.make_async_copy(source, target, isem.at[i])
        for i, (source, target) in enumerate(
            (
                (tk_in, tk_ref),
                (tv_in, tv_ref),
                (dest_in, dest_ref),
                (len_in, len_ref),
                (pk_in, pk_ref),
                (pv_in, pv_ref),
                (q_in, q_ref),
                (dq_in, dq_ref),
                (dk_in, dk_ref),
                (dv_in, dv_ref),
            )
        )
    ]
    for load in loads:
        load.start()

    barrier = pltpu.get_barrier_semaphore()
    for d in range(1, heads):
        other = lax.rem(tp + d, heads)
        pl.semaphore_signal(barrier, inc=1, device_id=(me, other), device_id_type=MESH)

    def greet(d, carry):
        pl.semaphore_signal(barrier, inc=1, device_id=(partner(d), tp), device_id_type=MESH)
        return carry

    lax.fori_loop(1, groups, greet, 0)

    rows = prompts * tokens * heads
    per_head = prompts * tokens
    row, column = iota((rows, rows), 0), iota((rows, rows), 1)
    wanted = lax.rem(row, per_head) * heads + lax.div(row, per_head)
    pick = jnp.where(column == wanted, 1.0, 0.0).astype(BF16)
    loads[0].wait()
    loads[1].wait()
    flat = jnp.concatenate([tk_ref[...].reshape(rows, hd), tv_ref[...].reshape(rows, hd)], axis=1)
    tsend[...] = dot(pick, flat).astype(BF16).reshape(heads, per_head, 2 * hd)

    loads[2].wait()
    dest_row = jnp.concatenate([dest_ref[p] for p in range(prompts)], axis=1)
    tab_v[...] = slot_table(dest_row, groups * SLOTS, blocks)
    table_copy = pltpu.make_async_copy(tab_v, tab_s, lsem.at[0])
    table_copy.start()

    pl.semaphore_wait(barrier, heads - 1 + groups - 1)

    tail_copies = []
    for d in range(1, heads):
        other = lax.rem(tp + d, heads)
        copy = pltpu.make_async_remote_copy(
            src_ref=tsend.at[other],
            dst_ref=trecv.at[tp],
            send_sem=tail_ssem.at[d],
            recv_sem=tail_rsem.at[d],
            device_id=(me, other),
            device_id_type=MESH,
        )
        copy.start()
        tail_copies.append(copy)
    own_tail = pltpu.make_async_copy(tsend.at[tp], trecv.at[tp], lsem.at[1])
    own_tail.start()
    wk[blocks] = jnp.zeros((BLOCK, hd), BF16)
    wv[blocks] = jnp.zeros((BLOCK, hd), BF16)
    table_copy.wait()
    for load in loads[3:6]:
        load.wait()
    own_tail.wait()
    for copy in tail_copies:
        copy.wait()

    for p in range(prompts):
        for s in range(heads):
            tail[p, s * tokens : (s + 1) * tokens] = trecv[s, p * tokens : (p + 1) * tokens]
    chunk = 128
    for p in range(prompts):
        start = len_ref[p] - tail_len
        for c in range(whole_len // chunk):
            row = iota((chunk, tail_len), 0) + c * chunk
            shift = jnp.where(iota((chunk, tail_len), 1) == row - start, 1.0, 0.0).astype(BF16)
            moved = dot(shift, tail[p])
            moved_k, moved_v = moved[:, :hd], moved[:, hd:]
            if c * chunk < prefix_len:
                early = iota((chunk, hd), 0) + c * chunk < start
                at = slice(c * chunk, (c + 1) * chunk)
                moved_k = jnp.where(early, pk_ref[p, at].astype(F32), moved_k)
                moved_v = jnp.where(early, pv_ref[p, at].astype(F32), moved_v)
            first = (p * whole_len + c * chunk) // BLOCK
            shape = (chunk // BLOCK, BLOCK, hd)
            wk[first : first + chunk // BLOCK] = moved_k.astype(BF16).reshape(shape)
            wv[first : first + chunk // BLOCK] = moved_v.astype(BF16).reshape(shape)

    def pack(target):
        for r in range(SLOTS):
            block = tab_s[0, target * SLOTS + r]
            send[target, 0, r] = wk[block]
            send[target, 1, r] = wv[block]

    def pool_copy(d):
        target = partner(d)
        return pltpu.make_async_remote_copy(
            src_ref=send.at[target],
            dst_ref=pool_ref.at[me],
            send_sem=ssem.at[d],
            recv_sem=rsem.at[d],
            device_id=(target, tp),
            device_id_type=MESH,
        )

    def ship(d, carry):
        pack(partner(d))
        pool_copy(d).start()
        return carry

    lax.fori_loop(1, groups, ship, 0)
    pack(me)
    own_pool = pltpu.make_async_copy(send.at[me], pool_ref.at[me], lsem.at[2])
    own_pool.start()

    for load in loads[6:]:
        load.wait()
    scale = 1.0 / math.sqrt(hd)
    chunk_tokens = 32
    chunk_rows = chunk_tokens * group
    for p in range(prompts):
        length = len_ref[p]

        def keys_of(whole):
            return whole[p * per_prompt : (p + 1) * per_prompt].reshape(whole_len, hd)

        def prefill(c, carry):
            first = pl.multiple_of(c * chunk_tokens, chunk_tokens)
            q = q_ref[p, pl.ds(first, chunk_tokens)].reshape(chunk_rows, hd)
            scores = dot_t(q, keys_of(wk)) * scale
            token = lax.div(iota((chunk_rows, whole_len), 0), group)
            last = length - tail_len + first + token
            scores = jnp.where(iota((chunk_rows, whole_len), 1) <= last, scores, -jnp.inf)
            peak = jnp.max(scores, axis=1, keepdims=True)
            weights = jnp.exp(scores - peak)
            total = jnp.sum(weights, axis=1, keepdims=True)
            summed = dot(weights.astype(BF16), keys_of(wv))
            result = (summed / total).astype(BF16)
            out_ref[p, pl.ds(first, chunk_tokens)] = result.reshape(chunk_tokens, group, hd)
            return carry

        lax.fori_loop(0, tail_len // chunk_tokens, prefill, 0)

        steps = dq_ref.shape[1]
        dq = dq_ref[p].reshape(steps * group, hd)
        scores = dot_t(dq, keys_of(wk)) * scale
        scores = jnp.where(iota(scores.shape, 1) < length, scores, -jnp.inf)
        fresh = dot_t(dq, dk_ref[p]) * scale
        step = lax.div(iota(fresh.shape, 0), group)
        fresh = jnp.where(iota(fresh.shape, 1) <= step, fresh, -jnp.inf)
        peak = jnp.maximum(
            jnp.max(scores, axis=1, keepdims=True), jnp.max(fresh, axis=1, keepdims=True)
        )
        weights = jnp.exp(scores - peak)
        fresh_weights = jnp.exp(fresh - peak)
        total = jnp.sum(weights, axis=1, keepdims=True) + jnp.sum(
            fresh_weights, axis=1, keepdims=True
        )
        summed = dot(weights.astype(BF16), keys_of(wv))
        summed = summed + dot(fresh_weights.astype(BF16), dv_ref[p])
        dout_ref[p] = (summed / total).astype(BF16).reshape(steps, group, hd)

    own_pool.wait()

    def finish(d, carry):
        pool_copy(d).wait()
        return carry

    lax.fori_loop(1, groups, finish, 0)


def store_kernel(pool_ref, out_ref, dout_ref, pk_ref, pv_ref, o_ref, do_ref, sem):
    copies = [
        pltpu.make_async_copy(pool_ref.at[:, 0], pk_ref, sem.at[0]),
        pltpu.make_async_copy(pool_ref.at[:, 1], pv_ref, sem.at[1]),
        pltpu.make_async_copy(out_ref, o_ref, sem.at[2]),
        pltpu.make_async_copy(dout_ref, do_ref, sem.at[3]),
    ]
    for copy in copies:
        copy.start()
    for copy in copies:
        copy.wait()


def per_device(groups, heads, tq, tk, tv, pk, pv, dq, dk, dv, lengths, dest):
    prompts, tail_len, group, hd = tq.shape
    tokens = tk.shape[1]
    prefix_len = pk.shape[1]
    steps = dq.shape[1]
    blocks = prompts * (prefix_len + tail_len) // BLOCK
    vmem = pl.BlockSpec(memory_space=pltpu.VMEM)
    hbm = pl.BlockSpec(memory_space=pltpu.HBM)
    shape = jax.ShapeDtypeStruct
    operands = (
        tk,
        tv,
        dest.reshape(prompts, 1, dest.shape[1]),
        lengths,
        pk.reshape(prompts, prefix_len, hd),
        pv.reshape(prompts, prefix_len, hd),
        tq,
        dq,
        dk.reshape(prompts, steps, hd),
        dv.reshape(prompts, steps, hd),
    )
    held = [pltpu.VMEM(x.shape, x.dtype) for x in operands]
    held[3] = pltpu.SMEM(lengths.shape, lengths.dtype)
    out, dout, pool = pl.pallas_call(
        functools.partial(exchange_kernel, groups, heads),
        out_shape=(
            pltpu.VMEM(tq.shape, BF16),
            pltpu.VMEM(dq.shape, BF16),
            pltpu.VMEM((groups, 2, SLOTS, BLOCK, hd), BF16),
        ),
        in_specs=[hbm] * len(operands),
        out_specs=(vmem, vmem, vmem),
        scratch_shapes=held
        + [
            pltpu.VMEM((heads, prompts * tokens, 2 * hd), BF16),
            pltpu.VMEM((heads, prompts * tokens, 2 * hd), BF16),
            pltpu.VMEM((prompts, tail_len, 2 * hd), BF16),
            pltpu.VMEM((blocks + 1, BLOCK, hd), BF16),
            pltpu.VMEM((blocks + 1, BLOCK, hd), BF16),
            pltpu.VMEM((groups, 2, SLOTS, BLOCK, hd), BF16),
            pltpu.VMEM((1, groups * SLOTS), jnp.int32),
            pltpu.SMEM((1, groups * SLOTS), jnp.int32),
            pltpu.SemaphoreType.DMA((heads,)),
            pltpu.SemaphoreType.DMA((heads,)),
            pltpu.SemaphoreType.DMA((groups,)),
            pltpu.SemaphoreType.DMA((groups,)),
            pltpu.SemaphoreType.DMA((3,)),
            pltpu.SemaphoreType.DMA((len(operands),)),
        ],
        compiler_params=pltpu.CompilerParams(
            collective_id=0, has_side_effects=True, vmem_limit_bytes=40 << 20
        ),
    )(*[pltpu.with_memory_space_constraint(x, pltpu.HBM) for x in operands])
    pool_k, pool_v, out, dout = pl.pallas_call(
        store_kernel,
        out_shape=(
            shape((groups, SLOTS, BLOCK, hd), BF16),
            shape((groups, SLOTS, BLOCK, hd), BF16),
            shape(tq.shape, BF16),
            shape(dq.shape, BF16),
        ),
        in_specs=[vmem] * 3,
        out_specs=(hbm,) * 4,
        scratch_shapes=[pltpu.SemaphoreType.DMA((4,))],
        compiler_params=pltpu.CompilerParams(vmem_limit_bytes=40 << 20),
    )(pool, out, dout)
    final = (1, groups * SLOTS, BLOCK, 1, hd)
    return out, dout, pool_k.reshape(final), pool_v.reshape(final)


def solution(mesh):
    in_specs = (
        P("req", None, "tp", None),
        P("req", "tp", None, None),
        P("req", "tp", None, None),
        P("req", None, "tp", None),
        P("req", None, "tp", None),
        P("req", None, "tp", None),
        P("req", None, "tp", None),
        P("req", None, "tp", None),
        P("req"),
        P("req", None, None),
    )
    out_specs = (
        P("req", None, "tp", None),
        P("req", None, "tp", None),
        P("req", None, None, "tp", None),
        P("req", None, None, "tp", None),
    )
    return jax.shard_map(
        functools.partial(per_device, mesh.shape["req"], mesh.shape["tp"]),
        mesh=mesh,
        in_specs=in_specs,
        out_specs=out_specs,
        check_vma=False,
    )
```

time: 207 us -> 121 us (0.58)
  Pallas kernels: 0 us -> 120 us
  waiting for transfers between devices: 73.2 us -> 0 us
  local copies, waits for them, and re-layouts: 51.8 us -> 0 us
  starting transfers between devices: 34.7 us -> 0 us
  other arithmetic: 34.2 us -> 0 us
  matrix products: 8.74 us -> 0 us
    pallas_call x0 -> x2, Pallas kernels: none -> 120 us  [the longest x1 118 us: per_device(): pl.pallas_call(functools.partial(exchange_kernel, groups, heads), out_sha...]
    all_to_all x4 -> x0, waiting for transfers between devices: 73.2 us -> none  [the longest x1 38.1 us: per_device(): lax.all_to_all(pack(whole_v), 'req', split_axis=0, concat_axis=0, tiled=T...]
    all_to_all x4 -> x0, starting transfers between devices: 34.7 us -> none  [the longest x1 18.7 us: per_device(): lax.all_to_all(pack(whole_k), 'req', split_axis=0, concat_axis=0, tiled=T...]
    scatter x14 -> x0, local copies, waits for them, and re-layouts: 28.8 us -> none  [the longest x2 26.4 us: pack(): return empty_slots.at[send_slot].set(blocks).reshape(groups_count, capaci...]
    scatter x9 -> x0, other arithmetic: 23.9 us -> none
    unnamed x23 -> x0, local copies, waits for them, and re-layouts: 12.6 us -> none
    dot_general x12 -> x0, matrix products: 8.74 us -> none  [the longest x2 4.4 us: prefill_one(): jnp.einsum('kgts,skd->tkgd', weights.astype(jnp.bfloat16), value_rows, pr...]
    reduce_sum x5 -> x0, other arithmetic: 4.01 us -> none  [the longest x2 3.48 us: prefill_one(): weight_sum = jnp.sum(weights, -1)]
  transfers between devices with their start and end apart: 4 -> 0, of which waited for: 2 -> 0; matrix products, arithmetic and copies ran while one was open for 29% -> 0% of each run, Pallas kernels for 0% -> 0%
where the time goes in v1:
time: 121 us; the launch traced here: 120 us
  Pallas kernels  120 us (99%)
    pallas_call x1, Pallas kernels, per_device(): pl.pallas_call(functools.partial(exchange_kernel, groups, heads), out_sha...  118 us

profile of v1, /device:TPU:24, one launch (start us, length us, event | category | flops | bytes accessed | tf_op | source)
XLA Modules:
  0.0 120.4 jit_solution(3989588233510971189)
XLA Ops:
  0.6 118.0 %shard_map.129 = (bf16[2,256,8,128]{3,2,1,0:T(8,128)(2,1)S(1)}, bf16[2,4,8,128]{3,2,1,0:T(8,128)(2,1)S(1)}, bf16[64,2,4,16,128]{4,3,2,1,0:T(8,128)(2,1)S(1)}) custom-call(bf16[2,32,8,128]{3,2,1,0:T(8,128)(2,1)} %tk_in.1, bf16[2,32,8,128]{3,2,1,0:T(8,128)(2,1)} %tv_in.1, s32[2,1,64]{2,1,0:T(1,128)} %bitcast.17, s32[2]{0:T(128)} %len_in.1, ...), custom_call_target="tpu_custom_call" | custom-call | tf_op jit(solution)/shard_map/pallas_call | solution.py:311
  118.7 1.7 %shard_map.130 = (bf16[64,4,16,128]{3,2,1,0:T(8,128)(2,1)}, bf16[64,4,16,128]{3,2,1,0:T(8,128)(2,1)}, bf16[2,256,8,128]{3,2,1,0:T(8,128)(2,1)}, bf16[2,4,8,128]{3,2,1,0:T(8,128)(2,1)}) custom-call(bf16[64,2,4,16,128]{4,3,2,1,0:T(8,128)(2,1)S(1)} %get-tuple-element.11.pool_ref, bf16[2,256,8,128]{3,2,1,0:T(8,128)(2,1)S(1)} %get-tuple-element.12.out_ref, ...), custom_call_target="tpu_custom_call" | custom-call | tf_op jit(solution)/shard_map/pallas_call | solution.py:341

commit v2 on v1

--- a/solution.py
+++ b/solution.py
@@ -67,8 +67,8 @@
     dk_ref,
     dv_ref,
     tsend,
-    trecv,
     tail,
+    shift,
     wk,
     wv,
     send,
@@ -78,7 +78,8 @@
     tail_rsem,
     ssem,
     rsem,
-    lsem,
+    tab_sem,
+    own_sem,
     isem,
 ):
     prompts, tail_len, group, hd = q_ref.shape
@@ -92,8 +93,10 @@
     nz = groups // Y
     my_y, my_z = me // nz, me % nz
 
-    def partner(d):
-        return lax.rem(my_y + d // nz, Y) * nz + lax.rem(my_z + d % nz, nz)
+    along_y = [lax.rem(my_y + dy, Y) * nz for dy in range(Y)]
+
+    def partner(dy, dz):
+        return along_y[dy] + lax.rem(my_z + dz, nz)
 
     loads = [
         pltpu.make_async_copy(source, target, isem.at[i])
@@ -112,7 +115,7 @@
             )
         )
     ]
-    for load in loads:
+    for load in loads[:3]:
         load.start()
 
     barrier = pltpu.get_barrier_semaphore()
@@ -120,101 +123,106 @@
         other = lax.rem(tp + d, heads)
         pl.semaphore_signal(barrier, inc=1, device_id=(me, other), device_id_type=MESH)
 
-    def greet(d, carry):
-        pl.semaphore_signal(barrier, inc=1, device_id=(partner(d), tp), device_id_type=MESH)
-        return carry
-
-    lax.fori_loop(1, groups, greet, 0)
+    for dy in range(Y):
+        for dz in range(nz):
+            if dy or dz:
+                pl.semaphore_signal(
+                    barrier, inc=1, device_id=(partner(dy, dz), tp), device_id_type=MESH
+                )
+    for load in loads[3:]:
+        load.start()
 
     rows = prompts * tokens * heads
     per_head = prompts * tokens
     row, column = iota((rows, rows), 0), iota((rows, rows), 1)
-    wanted = lax.rem(row, per_head) * heads + lax.div(row, per_head)
+    wanted = (row & (per_head - 1)) * heads + (row >> (per_head.bit_length() - 1))
     pick = jnp.where(column == wanted, 1.0, 0.0).astype(BF16)
     loads[0].wait()
     loads[1].wait()
     flat = jnp.concatenate([tk_ref[...].reshape(rows, hd), tv_ref[...].reshape(rows, hd)], axis=1)
-    tsend[...] = dot(pick, flat).astype(BF16).reshape(heads, per_head, 2 * hd)
+    picked = dot(pick, flat).astype(BF16)
+    for kv in range(2):
+        tsend[kv] = picked[:, kv * hd : (kv + 1) * hd].reshape(heads, prompts, tokens, hd)
+
+    pl.semaphore_wait(barrier, heads - 1 + groups - 1)
+
+    tail_copies = ([], [])
+    for kv in range(2):
+        here = tail.at[kv, :, pl.ds(tp * tokens, tokens)]
+        for d in range(1, heads):
+            other = lax.rem(tp + d, heads)
+            copy = pltpu.make_async_remote_copy(
+                src_ref=tsend.at[kv, other],
+                dst_ref=here,
+                send_sem=tail_ssem.at[kv, d],
+                recv_sem=tail_rsem.at[kv, d],
+                device_id=(me, other),
+                device_id_type=MESH,
+            )
+            copy.start()
+            tail_copies[kv].append(copy)
+        own = pltpu.make_async_copy(tsend.at[kv, tp], here, own_sem.at[kv])
+        own.start()
+        tail_copies[kv].append(own)
 
     loads[2].wait()
     dest_row = jnp.concatenate([dest_ref[p] for p in range(prompts)], axis=1)
     tab_v[...] = slot_table(dest_row, groups * SLOTS, blocks)
-    table_copy = pltpu.make_async_copy(tab_v, tab_s, lsem.at[0])
+    table_copy = pltpu.make_async_copy(tab_v, tab_s, tab_sem)
     table_copy.start()
-
-    pl.semaphore_wait(barrier, heads - 1 + groups - 1)
-
-    tail_copies = []
-    for d in range(1, heads):
-        other = lax.rem(tp + d, heads)
-        copy = pltpu.make_async_remote_copy(
-            src_ref=tsend.at[other],
-            dst_ref=trecv.at[tp],
-            send_sem=tail_ssem.at[d],
-            recv_sem=tail_rsem.at[d],
-            device_id=(me, other),
-            device_id_type=MESH,
-        )
-        copy.start()
-        tail_copies.append(copy)
-    own_tail = pltpu.make_async_copy(tsend.at[tp], trecv.at[tp], lsem.at[1])
-    own_tail.start()
+    chunk = tail_len
+    chunks = whole_len // chunk
+    loads[3].wait()
+    starts = [len_ref[p] - tail_len for p in range(prompts)]
+    distance = iota((chunk, tail_len), 0) - iota((chunk, tail_len), 1)
+    for p in range(prompts):
+        for c in range(chunks):
+            shift[p, c] = jnp.where(distance == starts[p] - c * chunk, 1.0, 0.0).astype(BF16)
     wk[blocks] = jnp.zeros((BLOCK, hd), BF16)
     wv[blocks] = jnp.zeros((BLOCK, hd), BF16)
     table_copy.wait()
-    for load in loads[3:6]:
-        load.wait()
-    own_tail.wait()
-    for copy in tail_copies:
-        copy.wait()
-
-    for p in range(prompts):
-        for s in range(heads):
-            tail[p, s * tokens : (s + 1) * tokens] = trecv[s, p * tokens : (p + 1) * tokens]
-    chunk = 128
-    for p in range(prompts):
-        start = len_ref[p] - tail_len
-        for c in range(whole_len // chunk):
-            row = iota((chunk, tail_len), 0) + c * chunk
-            shift = jnp.where(iota((chunk, tail_len), 1) == row - start, 1.0, 0.0).astype(BF16)
-            moved = dot(shift, tail[p])
-            moved_k, moved_v = moved[:, :hd], moved[:, hd:]
-            if c * chunk < prefix_len:
-                early = iota((chunk, hd), 0) + c * chunk < start
-                at = slice(c * chunk, (c + 1) * chunk)
-                moved_k = jnp.where(early, pk_ref[p, at].astype(F32), moved_k)
-                moved_v = jnp.where(early, pv_ref[p, at].astype(F32), moved_v)
-            first = (p * whole_len + c * chunk) // BLOCK
-            shape = (chunk // BLOCK, BLOCK, hd)
-            wk[first : first + chunk // BLOCK] = moved_k.astype(BF16).reshape(shape)
-            wv[first : first + chunk // BLOCK] = moved_v.astype(BF16).reshape(shape)
-
-    def pack(target):
-        for r in range(SLOTS):
-            block = tab_s[0, target * SLOTS + r]
-            send[target, 0, r] = wk[block]
-            send[target, 1, r] = wv[block]
-
-    def pool_copy(d):
-        target = partner(d)
-        return pltpu.make_async_remote_copy(
-            src_ref=send.at[target],
-            dst_ref=pool_ref.at[me],
-            send_sem=ssem.at[d],
-            recv_sem=rsem.at[d],
-            device_id=(target, tp),
-            device_id_type=MESH,
-        )
-
-    def ship(d, carry):
-        pack(partner(d))
-        pool_copy(d).start()
-        return carry
-
-    lax.fori_loop(1, groups, ship, 0)
-    pack(me)
-    own_pool = pltpu.make_async_copy(send.at[me], pool_ref.at[me], lsem.at[2])
-    own_pool.start()
+
+    local = []
+    for kv, (whole, prefix) in enumerate(((wk, pk_ref), (wv, pv_ref))):
+        loads[4 + kv].wait()
+        for copy in tail_copies[kv]:
+            copy.wait()
+        for p in range(prompts):
+            for c in range(chunks):
+                moved = dot(shift[p, c], tail[kv, p])
+                if c * chunk < prefix_len:
+                    early = iota((chunk, hd), 0) + c * chunk < starts[p]
+                    kept = prefix[p, c * chunk : (c + 1) * chunk].astype(F32)
+                    moved = jnp.where(early, kept, moved)
+                first = (p * whole_len + c * chunk) // BLOCK
+                whole[first : first + chunk // BLOCK] = moved.astype(BF16).reshape(
+                    chunk // BLOCK, BLOCK, hd
+                )
+
+        def pack(target):
+            for r in range(SLOTS):
+                send[kv, target, r] = whole[tab_s[0, target * SLOTS + r]]
+
+        for dy in range(Y):
+
+            def ship(dz, carry):
+                target = partner(dy, dz)
+                pack(target)
+                pltpu.make_async_remote_copy(
+                    src_ref=send.at[kv, target],
+                    dst_ref=pool_ref.at[kv, me],
+                    send_sem=ssem.at[kv],
+                    recv_sem=rsem.at[kv],
+                    device_id=(target, tp),
+                    device_id_type=MESH,
+                ).start()
+                return carry
+
+            lax.fori_loop(0 if dy else 1, nz, ship, 0)
+        pack(me)
+        own = pltpu.make_async_copy(send.at[kv, me], pool_ref.at[kv, me], own_sem.at[2 + kv])
+        own.start()
+        local.append(own)
 
     for load in loads[6:]:
         load.wait()
@@ -263,19 +271,26 @@
         summed = summed + dot(fresh_weights.astype(BF16), dv_ref[p])
         dout_ref[p] = (summed / total).astype(BF16).reshape(steps, group, hd)
 
-    own_pool.wait()
-
-    def finish(d, carry):
-        pool_copy(d).wait()
-        return carry
-
-    lax.fori_loop(1, groups, finish, 0)
+    for own in local:
+        own.wait()
+    for kv in range(2):
+        others = pl.ds(0, groups - 1)
+        every = pltpu.make_async_remote_copy(
+            src_ref=send.at[kv, others],
+            dst_ref=pool_ref.at[kv, others],
+            send_sem=ssem.at[kv],
+            recv_sem=rsem.at[kv],
+            device_id=(partner(0, 1), tp),
+            device_id_type=MESH,
+        )
+        every.wait_send()
+        every.wait_recv()
 
 
 def store_kernel(pool_ref, out_ref, dout_ref, pk_ref, pv_ref, o_ref, do_ref, sem):
     copies = [
-        pltpu.make_async_copy(pool_ref.at[:, 0], pk_ref, sem.at[0]),
-        pltpu.make_async_copy(pool_ref.at[:, 1], pv_ref, sem.at[1]),
+        pltpu.make_async_copy(pool_ref.at[0], pk_ref, sem.at[0]),
+        pltpu.make_async_copy(pool_ref.at[1], pv_ref, sem.at[1]),
         pltpu.make_async_copy(out_ref, o_ref, sem.at[2]),
         pltpu.make_async_copy(dout_ref, do_ref, sem.at[3]),
     ]
@@ -313,25 +328,26 @@
         out_shape=(
             pltpu.VMEM(tq.shape, BF16),
             pltpu.VMEM(dq.shape, BF16),
-            pltpu.VMEM((groups, 2, SLOTS, BLOCK, hd), BF16),
+            pltpu.VMEM((2, groups, SLOTS, BLOCK, hd), BF16),
         ),
         in_specs=[hbm] * len(operands),
         out_specs=(vmem, vmem, vmem),
         scratch_shapes=held
         + [
-            pltpu.VMEM((heads, prompts * tokens, 2 * hd), BF16),
-            pltpu.VMEM((heads, prompts * tokens, 2 * hd), BF16),
-            pltpu.VMEM((prompts, tail_len, 2 * hd), BF16),
+            pltpu.VMEM((2, heads, prompts, tokens, hd), BF16),
+            pltpu.VMEM((2, prompts, tail_len, hd), BF16),
+            pltpu.VMEM((prompts, (prefix_len + tail_len) // tail_len, tail_len, tail_len), BF16),
             pltpu.VMEM((blocks + 1, BLOCK, hd), BF16),
             pltpu.VMEM((blocks + 1, BLOCK, hd), BF16),
-            pltpu.VMEM((groups, 2, SLOTS, BLOCK, hd), BF16),
+            pltpu.VMEM((2, groups, SLOTS, BLOCK, hd), BF16),
             pltpu.VMEM((1, groups * SLOTS), jnp.int32),
             pltpu.SMEM((1, groups * SLOTS), jnp.int32),
-            pltpu.SemaphoreType.DMA((heads,)),
-            pltpu.SemaphoreType.DMA((heads,)),
-            pltpu.SemaphoreType.DMA((groups,)),
-            pltpu.SemaphoreType.DMA((groups,)),
-            pltpu.SemaphoreType.DMA((3,)),
+            pltpu.SemaphoreType.DMA((2, heads)),
+            pltpu.SemaphoreType.DMA((2, heads)),
+            pltpu.SemaphoreType.DMA((2,)),
+            pltpu.SemaphoreType.DMA((2,)),
+            pltpu.SemaphoreType.DMA,
+            pltpu.SemaphoreType.DMA((4,)),
             pltpu.SemaphoreType.DMA((len(operands),)),
         ],
         compiler_params=pltpu.CompilerParams(

time: 121 us -> 118 us (0.975)
  Pallas kernels: 120 us -> 117 us
    pallas_call x1, Pallas kernels: 118 us -> 116 us  [per_device(): pl.pallas_call(functools.partial(exchange_kernel, groups, heads), out_sha...]
where the time goes in v2:
time: 118 us
  Pallas kernels  117 us (99%)
    pallas_call x1, Pallas kernels, per_device(): pl.pallas_call(functools.partial(exchange_kernel, groups, heads), out_sha...  116 us

profile of v2, /device:TPU:24, one launch (start us, length us, event | category | flops | bytes accessed | tf_op | source)
XLA Modules:
  0.0 118.1 jit_solution(6064608463384136998)
XLA Ops:
  0.6 115.7 %shard_map.129 = (bf16[2,256,8,128]{3,2,1,0:T(8,128)(2,1)S(1)}, bf16[2,4,8,128]{3,2,1,0:T(8,128)(2,1)S(1)}, bf16[2,64,4,16,128]{4,3,2,1,0:T(8,128)(2,1)S(1)}) custom-call(bf16[2,32,8,128]{3,2,1,0:T(8,128)(2,1)} %tk_in.1, bf16[2,32,8,128]{3,2,1,0:T(8,128)(2,1)} %tv_in.1, s32[2,1,64]{2,1,0:T(1,128)} %bitcast.17, s32[2]{0:T(128)} %len_in.1, ...), custom_call_target="tpu_custom_call" | custom-call | tf_op jit(solution)/shard_map/pallas_call | solution.py:326
  116.4 1.7 %shard_map.130 = (bf16[64,4,16,128]{3,2,1,0:T(8,128)(2,1)}, bf16[64,4,16,128]{3,2,1,0:T(8,128)(2,1)}, bf16[2,256,8,128]{3,2,1,0:T(8,128)(2,1)}, bf16[2,4,8,128]{3,2,1,0:T(8,128)(2,1)}) custom-call(bf16[2,64,4,16,128]{4,3,2,1,0:T(8,128)(2,1)S(1)} %get-tuple-element.11.pool_ref, bf16[2,256,8,128]{3,2,1,0:T(8,128)(2,1)S(1)} %get-tuple-element.12.out_ref, ...), custom_call_target="tpu_custom_call" | custom-call | tf_op jit(solution)/shard_map/pallas_call | solution.py:357

commit v3 on v2

--- a/solution.py
+++ b/solution.py
@@ -137,18 +137,15 @@
     row, column = iota((rows, rows), 0), iota((rows, rows), 1)
     wanted = (row & (per_head - 1)) * heads + (row >> (per_head.bit_length() - 1))
     pick = jnp.where(column == wanted, 1.0, 0.0).astype(BF16)
-    loads[0].wait()
-    loads[1].wait()
-    flat = jnp.concatenate([tk_ref[...].reshape(rows, hd), tv_ref[...].reshape(rows, hd)], axis=1)
-    picked = dot(pick, flat).astype(BF16)
-    for kv in range(2):
-        tsend[kv] = picked[:, kv * hd : (kv + 1) * hd].reshape(heads, prompts, tokens, hd)
-
-    pl.semaphore_wait(barrier, heads - 1 + groups - 1)
-
-    tail_copies = ([], [])
-    for kv in range(2):
+
+    def order_by_head(kv, source):
+        loads[kv].wait()
+        picked = dot(pick, source[...].reshape(rows, hd)).astype(BF16)
+        tsend[kv] = picked.reshape(heads, prompts, tokens, hd)
+
+    def send_tails(kv):
         here = tail.at[kv, :, pl.ds(tp * tokens, tokens)]
+        copies = []
         for d in range(1, heads):
             other = lax.rem(tp + d, heads)
             copy = pltpu.make_async_remote_copy(
@@ -160,10 +157,16 @@
                 device_id_type=MESH,
             )
             copy.start()
-            tail_copies[kv].append(copy)
+            copies.append(copy)
         own = pltpu.make_async_copy(tsend.at[kv, tp], here, own_sem.at[kv])
         own.start()
-        tail_copies[kv].append(own)
+        return copies + [own]
+
+    order_by_head(0, tk_ref)
+    pl.semaphore_wait(barrier, heads - 1 + groups - 1)
+    tail_copies = [send_tails(0)]
+    order_by_head(1, tv_ref)
+    tail_copies.append(send_tails(1))
 
     loads[2].wait()
     dest_row = jnp.concatenate([dest_ref[p] for p in range(prompts)], axis=1)
@@ -203,7 +206,7 @@
             for r in range(SLOTS):
                 send[kv, target, r] = whole[tab_s[0, target * SLOTS + r]]
 
-        for dy in range(Y):
+        for dy in (2, 1, 3, 0):
 
             def ship(dz, carry):
                 target = partner(dy, dz)

time: 118 us -> 118 us (level); the launches traced: 118 us -> 116 us
    pallas_call x1, Pallas kernels: 116 us -> 114 us  [per_device(): pl.pallas_call(functools.partial(exchange_kernel, groups, heads), out_sha...]
where the time goes in v3:
time: 118 us; the launch traced here: 116 us
  Pallas kernels  116 us (98%)
    pallas_call x1, Pallas kernels, per_device(): pl.pallas_call(functools.partial(exchange_kernel, groups, heads), out_sha...  114 us

profile of v3, /device:TPU:24, one launch (start us, length us, event | category | flops | bytes accessed | tf_op | source)
XLA Modules:
  0.0 116.4 jit_solution(6709517781120816642)
XLA Ops:
  0.6 114.0 %shard_map.129 = (bf16[2,256,8,128]{3,2,1,0:T(8,128)(2,1)S(1)}, bf16[2,4,8,128]{3,2,1,0:T(8,128)(2,1)S(1)}, bf16[2,64,4,16,128]{4,3,2,1,0:T(8,128)(2,1)S(1)}) custom-call(bf16[2,32,8,128]{3,2,1,0:T(8,128)(2,1)} %tk_in.1, bf16[2,32,8,128]{3,2,1,0:T(8,128)(2,1)} %tv_in.1, s32[2,1,64]{2,1,0:T(1,128)} %bitcast.17, s32[2]{0:T(128)} %len_in.1, ...), custom_call_target="tpu_custom_call" | custom-call | tf_op jit(solution)/shard_map/pallas_call | solution.py:329
  114.7 1.7 %shard_map.130 = (bf16[64,4,16,128]{3,2,1,0:T(8,128)(2,1)}, bf16[64,4,16,128]{3,2,1,0:T(8,128)(2,1)}, bf16[2,256,8,128]{3,2,1,0:T(8,128)(2,1)}, bf16[2,4,8,128]{3,2,1,0:T(8,128)(2,1)}) custom-call(bf16[2,64,4,16,128]{4,3,2,1,0:T(8,128)(2,1)S(1)} %get-tuple-element.11.pool_ref, bf16[2,256,8,128]{3,2,1,0:T(8,128)(2,1)S(1)} %get-tuple-element.12.out_ref, ...), custom_call_target="tpu_custom_call" | custom-call | tf_op jit(solution)/shard_map/pallas_call | solution.py:360

commit v4 on v3

--- a/solution.py
+++ b/solution.py
@@ -163,16 +163,16 @@
         return copies + [own]
 
     order_by_head(0, tk_ref)
-    pl.semaphore_wait(barrier, heads - 1 + groups - 1)
-    tail_copies = [send_tails(0)]
-    order_by_head(1, tv_ref)
-    tail_copies.append(send_tails(1))
-
     loads[2].wait()
     dest_row = jnp.concatenate([dest_ref[p] for p in range(prompts)], axis=1)
     tab_v[...] = slot_table(dest_row, groups * SLOTS, blocks)
     table_copy = pltpu.make_async_copy(tab_v, tab_s, tab_sem)
     table_copy.start()
+    pl.semaphore_wait(barrier, heads - 1 + groups - 1)
+    tail_copies = [send_tails(0)]
+    order_by_head(1, tv_ref)
+    tail_copies.append(send_tails(1))
+
     chunk = tail_len
     chunks = whole_len // chunk
     loads[3].wait()

time: 118 us -> 118 us (level)
  no operation moved by 1% of the time
where the time goes in v4:
time: 118 us; the launch traced here: 116 us
  Pallas kernels  116 us (98%)
    pallas_call x1, Pallas kernels, per_device(): pl.pallas_call(functools.partial(exchange_kernel, groups, heads), out_sha...  114 us

profile of v4, /device:TPU:24, one launch (start us, length us, event | category | flops | bytes accessed | tf_op | source)
XLA Modules:
  0.0 116.4 jit_solution(1905526095787325399)
XLA Ops:
  0.6 114.0 %shard_map.129 = (bf16[2,256,8,128]{3,2,1,0:T(8,128)(2,1)S(1)}, bf16[2,4,8,128]{3,2,1,0:T(8,128)(2,1)S(1)}, bf16[2,64,4,16,128]{4,3,2,1,0:T(8,128)(2,1)S(1)}) custom-call(bf16[2,32,8,128]{3,2,1,0:T(8,128)(2,1)} %tk_in.1, bf16[2,32,8,128]{3,2,1,0:T(8,128)(2,1)} %tv_in.1, s32[2,1,64]{2,1,0:T(1,128)} %bitcast.17, s32[2]{0:T(128)} %len_in.1, ...), custom_call_target="tpu_custom_call" | custom-call | tf_op jit(solution)/shard_map/pallas_call | solution.py:329
  114.7 1.7 %shard_map.130 = (bf16[64,4,16,128]{3,2,1,0:T(8,128)(2,1)}, bf16[64,4,16,128]{3,2,1,0:T(8,128)(2,1)}, bf16[2,256,8,128]{3,2,1,0:T(8,128)(2,1)}, bf16[2,4,8,128]{3,2,1,0:T(8,128)(2,1)}) custom-call(bf16[2,64,4,16,128]{4,3,2,1,0:T(8,128)(2,1)S(1)} %get-tuple-element.11.pool_ref, bf16[2,256,8,128]{3,2,1,0:T(8,128)(2,1)S(1)} %get-tuple-element.12.out_ref, ...), custom_call_target="tpu_custom_call" | custom-call | tf_op jit(solution)/shard_map/pallas_call | solution.py:360
